TPU v7x, 32 devices: a whole 2x2x4 slice. The times are simulated.
32 devices in a mesh: tm: 16 (over z, y, x), state: 2 (over core).
Axes of the slice: x: 2, y: 2, z: 4, core: 2. Of those that a mesh axis runs over, the one named last changes fastest.
Arguments:
- features: float32 [4, 256, 512], P(None, 'tm'), may hold values from -18 to 18
- gauss_means: float32 [1024, 512], P('state'), may hold values from -3 to 3
- precisions: float32 [1024, 512], P('state'), may hold values from 0.5 to 2
- transitions: bfloat16 [1024, 1024], P('state'), may hold values from 0 to 1, as said below
- initial: bfloat16 [1024], P('state'), may hold values from 0.099609375 to 10
- reset_flags: int32 [4, 256], P(None, 'tm'), may hold values from 0 to 1, as said below
Outputs:
- posteriors: bfloat16 [4, 256, 1024], P(None, 'tm', 'state')
- evidence: float32 [4, 256], P(None, ('tm', 'state'))
Inputs may be any that keep to these rules, and one draw needn't show every extreme that they name: `transitions`: every entry nonnegative; each row sums to 1 up to the rounding of its entries; the diagonal holds half or more of each row. reset_flags[b, 0] = 1 in every stream; the runs of frames from one 1 to the next (utterances) hold 1 to 16 frames, and some hold exactly 16.
All inputs are finite; a program needn't handle non-finite values.
Results may differ from a plain program's by a relative error of at most 0.012.
Values may be sent and summed in bfloat16 or wider, within the bound.
A program may use at most 64 MiB of HBM per device.

v0:
```python
import jax
import jax.numpy as jnp
from jax import lax
from jax.sharding import PartitionSpec as P

SPAN = 1


acoustic = 0.1


def passed_along(block, axis, distance):
    devices = range(lax.axis_size(axis))
    route = [(i - distance, i) for i in devices if i - distance in devices]
    return lax.ppermute(block, axis, route)


def local_scores(features, gauss_means, precisions):
    streams, frames, feat_width = features.shape
    highest = lax.Precision.HIGHEST
    flat_feats = features.reshape(streams * frames, feat_width)
    quadratic = jnp.dot(flat_feats * flat_feats, (-0.5 * precisions).T, precision=highest)
    linear_part = jnp.dot(flat_feats, (precisions * gauss_means).T, precision=highest)
    offset = 0.5 * jnp.sum(jnp.log(precisions) - precisions * gauss_means * gauss_means, axis=1)
    return (acoustic * (quadratic + linear_part + offset)).reshape(
        streams, frames, gauss_means.shape[0]
    )


def run_block(emission_t, reset_t, trans, trans_back, prior_dist, alpha_in, beta_in):
    states = trans.shape[0]

    def forward_step(alpha_prev, inputs):
        emit_row, reset_row = inputs
        predicted = jnp.dot(
            alpha_prev.astype(jnp.bfloat16), trans, preferred_element_type=jnp.float32
        )
        predicted = jnp.where(reset_row[:, None] == 1, prior_dist[None, :], predicted)
        weighted = emit_row * predicted
        norm_total = jnp.sum(weighted, axis=1)
        alpha_next = weighted / norm_total[:, None]
        return (alpha_next, (alpha_next, jnp.log(norm_total)))

    alpha_out, (alphas, log_norms) = lax.scan(forward_step, alpha_in, (emission_t, reset_t))

    def backward_step(beta_next, inputs):
        emit_row, reset_row = inputs
        spread = jnp.dot(
            (emit_row * beta_next).astype(jnp.bfloat16),
            trans_back,
            preferred_element_type=jnp.float32,
        )
        spread = spread / jnp.sum(spread, axis=1, keepdims=True)
        beta_prev = jnp.where(reset_row[:, None] == 1, 1.0 / states, spread)
        return (beta_prev, beta_next)

    beta_out, betas = lax.scan(backward_step, beta_in, (emission_t, reset_t), reverse=True)
    return (alpha_out, alphas, log_norms, beta_out, betas)


def run_chain(scores, resets, trans, trans_back, prior_dist, relay_step, relays):
    maxima = jnp.max(scores, axis=2, keepdims=True)
    emission_t = jnp.swapaxes(jnp.exp(scores - maxima), 0, 1)
    reset_t = jnp.swapaxes(resets, 0, 1)
    streams, states = (scores.shape[0], scores.shape[2])
    alpha_in = jnp.full((streams, states), 1.0 / states, jnp.float32)
    beta_in = alpha_in
    for relay_turn in range(relays + 1):
        alpha_out, alphas, log_norms, beta_out, betas = run_block(
            emission_t, reset_t, trans, trans_back, prior_dist, alpha_in, beta_in
        )
        if relay_turn < relays:
            alpha_in, beta_in = relay_step(alpha_out, beta_out)
    product = alphas * betas
    posterior = (product / jnp.sum(product, axis=2, keepdims=True)).astype(jnp.bfloat16)
    return (jnp.swapaxes(posterior, 0, 1), jnp.swapaxes(log_norms, 0, 1))


def per_device(features, gauss_means, precisions, transitions, initial, reset_flags):
    trans, prior_raw = (
        lax.all_gather(transitions, "state", axis=0, tiled=True),
        lax.all_gather(initial, "state", axis=0, tiled=True),
    )
    trans_back = trans.T
    states = trans.shape[0]
    prior_float = prior_raw.astype(jnp.float32)
    prior_dist = prior_float / jnp.sum(prior_float)
    scores = local_scores(features, gauss_means, precisions)
    group = lax.axis_size("state")
    place = lax.axis_index("state")
    blocks = lax.axis_size("tm")
    block_place = lax.axis_index("tm")
    quarter = features.shape[1] // group
    is_last = block_place * group + place == blocks * group - 1

    def relay_step(alpha_out, beta_out):
        alpha_next = passed_along(alpha_out, ("tm", "state"), 1)
        beta_next = passed_along(beta_out, ("tm", "state"), -1)
        beta_next = jnp.where(is_last, 1.0 / states, beta_next)
        return (alpha_next, beta_next)

    my_scores = lax.all_to_all(scores, "state", split_axis=1, concat_axis=2, tiled=True)
    my_flags = lax.dynamic_slice_in_dim(reset_flags, place * quarter, quarter, 1)
    posterior, evidence = run_chain(
        my_scores, my_flags, trans, trans_back, prior_dist, relay_step, SPAN * group
    )
    posteriors = lax.all_to_all(posterior, "state", split_axis=2, concat_axis=1, tiled=True)
    return (posteriors, evidence)


def solution(mesh):
    return jax.shard_map(
        per_device,
        mesh=mesh,
        in_specs=(
            P(None, "tm", None),
            P("state", None),
            P("state", None),
            P("state", None),
            P("state"),
            P(None, "tm"),
        ),
        out_specs=(P(None, "tm", "state"), P(None, ("tm", "state"))),
        check_vma=False,
    )
```

profile of v0, /device:TPU:7, one launch (start us, length us, event | category | flops | bytes accessed | tf_op | source)
XLA Modules:
  0.0 140.5 jit_solution(5319305410752097633)
XLA Ops:
  7.2 2.4 %copy.41 = bf16[512,1024]{0,1:T(8,128)(2,1)} copy(bf16[512,1024]{1,0:T(8,128)(2,1)} %param.21) | data formatting | bytes 2097152 | tf_op args[3]
  10.0 0.6 copy-done.4
  10.6 1.1 fusion.30
  11.6 1.2 fusion.27
  12.8 0.7 copy.38
  13.6 4.0 %all-to-all-start = ((f32[4,16,512]{2,0,1:T(4,128)}), f32[4,16,512]{2,0,1:T(4,128)S(1)}, u32[]{:S(2)}, u32[]{:S(2)}) async-start(f32[4,16,512]{2,0,1:T(4,128)} %copy.38), calls=%async_computation | async-start | bytes 262144 | tf_op jit(solution)/shard_map/all_to_all | solution.py:102
  17.8 0.9 all-to-all-done
  18.8 1.8 %all-gather = bf16[2,1,512]{2,1,0:T(2,128)(2,1)S(1)} all-gather(bf16[1,1,512]{2,1,0:T(2,128)(2,1)S(1)} %reshape.112), channel_id=1, replica_groups=mesh['tm'=16,'state'=2] {'state'}, dimensions={0}, use_global_device_ids=true | all-gather | bytes 3072 | tf_op jit(solution)/shard_map/all_gather | solution.py:82
  20.7 0.7 convert_reduce_fusion
  21.4 0.7 convert_divide_fusion
  22.3 17.5 %while.85 = (s32[]{:T(128)}, f32[4,1024]{1,0:T(4,128)S(1)}, s32[8,4]{1,0:T(8,128)S(1)}, f32[8,4,1024]{2,1,0:T(4,128)S(1)}, bf16[1024,1024]{1,0:T(8,128)(2,1)}, /*index=5*/s32[]{:T(128)}, s32[]{:T(128)}, s32[]{:T(128)}) while((s32[]{:T(128)}, f32[4,1024]{1,0:T(4,128)S(1)}, s32[8,4]{1,0:T(8,128)S(1)}, ...), condition=%wide.region_14.15_spmd.clone, body=%wide.region_12.14_spmd.clone.sunk | while | flops 8413188 | bytes 2179251 | solution.py:57
  22.4 2.1 %fusion.76 = (f32[4]{0:T(128)S(1)}, f32[4,1024]{1,0:T(4,128)S(1)}) fusion(bf16[1024,1024]{1,0:T(8,128)(2,1)} %get-tuple-element.988, f32[4,1024]{1,0:T(4,128)S(1)} %get-tuple-element.977, f32[8,4,1024]{2,1,0:T(4,128)S(1)} %get-tuple-element.987, s32[]{:T(128)S(6)} %sub.44, pred[]{:T(512)S(6)} %compare.7), kind=kOutput, calls=%fused_computation.71.clone.1 | convolution fusion | flops 8404988 | bytes 2146325 | tf_op jit(solution)/shard_map/while/body/eval_jaxpr/dot_general | solution.py:48
  24.5 2.1 %fusion.76 = (f32[4]{0:T(128)S(1)}, f32[4,1024]{1,0:T(4,128)S(1)}) fusion(bf16[1024,1024]{1,0:T(8,128)(2,1)} %get-tuple-element.988, f32[4,1024]{1,0:T(4,128)S(1)} %get-tuple-element.977, f32[8,4,1024]{2,1,0:T(4,128)S(1)} %get-tuple-element.987, s32[]{:T(128)S(6)} %sub.44, pred[]{:T(512)S(6)} %compare.7), kind=kOutput, calls=%fused_computation.71.clone.1 | convolution fusion | flops 8404988 | bytes 2146325 | tf_op jit(solution)/shard_map/while/body/eval_jaxpr/dot_general | solution.py:48
  26.7 2.1 %fusion.76 = (f32[4]{0:T(128)S(1)}, f32[4,1024]{1,0:T(4,128)S(1)}) fusion(bf16[1024,1024]{1,0:T(8,128)(2,1)} %get-tuple-element.988, f32[4,1024]{1,0:T(4,128)S(1)} %get-tuple-element.977, f32[8,4,1024]{2,1,0:T(4,128)S(1)} %get-tuple-element.987, s32[]{:T(128)S(6)} %sub.44, pred[]{:T(512)S(6)} %compare.7), kind=kOutput, calls=%fused_computation.71.clone.1 | convolution fusion | flops 8404988 | bytes 2146325 | tf_op jit(solution)/shard_map/while/body/eval_jaxpr/dot_general | solution.py:48
  28.9 2.1 %fusion.76 = (f32[4]{0:T(128)S(1)}, f32[4,1024]{1,0:T(4,128)S(1)}) fusion(bf16[1024,1024]{1,0:T(8,128)(2,1)} %get-tuple-element.988, f32[4,1024]{1,0:T(4,128)S(1)} %get-tuple-element.977, f32[8,4,1024]{2,1,0:T(4,128)S(1)} %get-tuple-element.987, s32[]{:T(128)S(6)} %sub.44, pred[]{:T(512)S(6)} %compare.7), kind=kOutput, calls=%fused_computation.71.clone.1 | convolution fusion | flops 8404988 | bytes 2146325 | tf_op jit(solution)/shard_map/while/body/eval_jaxpr/dot_general | solution.py:48
  31.1 2.1 %fusion.76 = (f32[4]{0:T(128)S(1)}, f32[4,1024]{1,0:T(4,128)S(1)}) fusion(bf16[1024,1024]{1,0:T(8,128)(2,1)} %get-tuple-element.988, f32[4,1024]{1,0:T(4,128)S(1)} %get-tuple-element.977, f32[8,4,1024]{2,1,0:T(4,128)S(1)} %get-tuple-element.987, s32[]{:T(128)S(6)} %sub.44, pred[]{:T(512)S(6)} %compare.7), kind=kOutput, calls=%fused_computation.71.clone.1 | convolution fusion | flops 8404988 | bytes 2146325 | tf_op jit(solution)/shard_map/while/body/eval_jaxpr/dot_general | solution.py:48
  33.3 2.1 %fusion.76 = (f32[4]{0:T(128)S(1)}, f32[4,1024]{1,0:T(4,128)S(1)}) fusion(bf16[1024,1024]{1,0:T(8,128)(2,1)} %get-tuple-element.988, f32[4,1024]{1,0:T(4,128)S(1)} %get-tuple-element.977, f32[8,4,1024]{2,1,0:T(4,128)S(1)} %get-tuple-element.987, s32[]{:T(128)S(6)} %sub.44, pred[]{:T(512)S(6)} %compare.7), kind=kOutput, calls=%fused_computation.71.clone.1 | convolution fusion | flops 8404988 | bytes 2146325 | tf_op jit(solution)/shard_map/while/body/eval_jaxpr/dot_general | solution.py:48
  35.5 2.1 %fusion.76 = (f32[4]{0:T(128)S(1)}, f32[4,1024]{1,0:T(4,128)S(1)}) fusion(bf16[1024,1024]{1,0:T(8,128)(2,1)} %get-tuple-element.988, f32[4,1024]{1,0:T(4,128)S(1)} %get-tuple-element.977, f32[8,4,1024]{2,1,0:T(4,128)S(1)} %get-tuple-element.987, s32[]{:T(128)S(6)} %sub.44, pred[]{:T(512)S(6)} %compare.7), kind=kOutput, calls=%fused_computation.71.clone.1 | convolution fusion | flops 8404988 | bytes 2146325 | tf_op jit(solution)/shard_map/while/body/eval_jaxpr/dot_general | solution.py:48
  37.7 2.1 %fusion.76 = (f32[4]{0:T(128)S(1)}, f32[4,1024]{1,0:T(4,128)S(1)}) fusion(bf16[1024,1024]{1,0:T(8,128)(2,1)} %get-tuple-element.988, f32[4,1024]{1,0:T(4,128)S(1)} %get-tuple-element.977, f32[8,4,1024]{2,1,0:T(4,128)S(1)} %get-tuple-element.987, s32[]{:T(128)S(6)} %sub.44, pred[]{:T(512)S(6)} %compare.7), kind=kOutput, calls=%fused_computation.71.clone.1 | convolution fusion | flops 8404988 | bytes 2146325 | tf_op jit(solution)/shard_map/while/body/eval_jaxpr/dot_general | solution.py:48
  39.9 2.1 %collective-permute-start.2 = (f32[4,1024]{1,0:T(4,128)S(1)}, f32[4,1024]{1,0:T(4,128)S(1)}, u32[]{:S(2)}, u32[]{:S(2)}) collective-permute-start(f32[4,1024]{1,0:T(4,128)S(1)} %get-tuple-element.440), channel_id=1, source_target_pairs={{1,0},{2,1},{3,2},{4,3},{5,4},{6,5},{7,6},{8,7},{9,8},{10,9},{11,1... | collective-permute-start | bytes 49160 | tf_op jit(solution)/shard_map/ppermute | solution.py:15
  42.0 4.0 %copy.42 = bf16[1024,1024]{1,0:T(8,128)(2,1)} copy(bf16[1024,1024]{0,1:T(8,128)(2,1)} %bitcast.117) | data formatting | bytes 4194304
  46.0 17.7 %while.84 = (s32[]{:T(128)}, f32[4,1024]{1,0:T(4,128)S(1)}, f32[8,4,1024]{2,1,0:T(4,128)S(1)}, s32[8,4]{1,0:T(8,128)S(1)}, f32[1024]{0:T(1024)S(1)}, /*index=5*/bf16[1024,1024]{1,0:T(8,128)(2,1)}, s32[]{:T(128)}, s32[]{:T(128)}) while((s32[]{:T(128)}, f32[4,1024]{1,0:T(4,128)S(1)}, f32[8,4,1024]{2,1,0:T(4,128)S(1)}, ...), condition=%wide.region_5.6_spmd.clone, body=%wide.region_3.5_spmd.clone.sunk | while | flops 8409091 | bytes 2183335 | solution.py:44
  46.0 2.2 %fusion.74 = (f32[4]{0:T(128)S(1)}, f32[4,1024]{1,0:T(4,128)S(1)}) fusion(bf16[1024,1024]{1,0:T(8,128)(2,1)} %get-tuple-element.914, f32[4,1024]{1,0:T(4,128)S(1)} %get-tuple-element.902, pred[]{:T(512)S(6)} %compare.6, f32[1024]{0:T(1024)S(1)} %get-tuple-element.913, pred[4]{0:T(512)(128)(4,1)S(1)} %compare_bitcast_fusion.16, ...), kind=kOutput, calls=%fused_computation.70.clone.1 | convolution fusion | flops 8404988 | bytes 2150425 | tf_op jit(solution)/shard_map/while/body/eval_jaxpr/dot_general | solution.py:35
  48.3 2.1 %fusion.74 = (f32[4]{0:T(128)S(1)}, f32[4,1024]{1,0:T(4,128)S(1)}) fusion(bf16[1024,1024]{1,0:T(8,128)(2,1)} %get-tuple-element.914, f32[4,1024]{1,0:T(4,128)S(1)} %get-tuple-element.902, pred[]{:T(512)S(6)} %compare.6, f32[1024]{0:T(1024)S(1)} %get-tuple-element.913, pred[4]{0:T(512)(128)(4,1)S(1)} %compare_bitcast_fusion.16, ...), kind=kOutput, calls=%fused_computation.70.clone.1 | convolution fusion | flops 8404988 | bytes 2150425 | tf_op jit(solution)/shard_map/while/body/eval_jaxpr/dot_general | solution.py:35
  50.5 2.1 %fusion.74 = (f32[4]{0:T(128)S(1)}, f32[4,1024]{1,0:T(4,128)S(1)}) fusion(bf16[1024,1024]{1,0:T(8,128)(2,1)} %get-tuple-element.914, f32[4,1024]{1,0:T(4,128)S(1)} %get-tuple-element.902, pred[]{:T(512)S(6)} %compare.6, f32[1024]{0:T(1024)S(1)} %get-tuple-element.913, pred[4]{0:T(512)(128)(4,1)S(1)} %compare_bitcast_fusion.16, ...), kind=kOutput, calls=%fused_computation.70.clone.1 | convolution fusion | flops 8404988 | bytes 2150425 | tf_op jit(solution)/shard_map/while/body/eval_jaxpr/dot_general | solution.py:35
  52.7 2.1 %fusion.74 = (f32[4]{0:T(128)S(1)}, f32[4,1024]{1,0:T(4,128)S(1)}) fusion(bf16[1024,1024]{1,0:T(8,128)(2,1)} %get-tuple-element.914, f32[4,1024]{1,0:T(4,128)S(1)} %get-tuple-element.902, pred[]{:T(512)S(6)} %compare.6, f32[1024]{0:T(1024)S(1)} %get-tuple-element.913, pred[4]{0:T(512)(128)(4,1)S(1)} %compare_bitcast_fusion.16, ...), kind=kOutput, calls=%fused_computation.70.clone.1 | convolution fusion | flops 8404988 | bytes 2150425 | tf_op jit(solution)/shard_map/while/body/eval_jaxpr/dot_general | solution.py:35
  54.9 2.1 %fusion.74 = (f32[4]{0:T(128)S(1)}, f32[4,1024]{1,0:T(4,128)S(1)}) fusion(bf16[1024,1024]{1,0:T(8,128)(2,1)} %get-tuple-element.914, f32[4,1024]{1,0:T(4,128)S(1)} %get-tuple-element.902, pred[]{:T(512)S(6)} %compare.6, f32[1024]{0:T(1024)S(1)} %get-tuple-element.913, pred[4]{0:T(512)(128)(4,1)S(1)} %compare_bitcast_fusion.16, ...), kind=kOutput, calls=%fused_computation.70.clone.1 | convolution fusion | flops 8404988 | bytes 2150425 | tf_op jit(solution)/shard_map/while/body/eval_jaxpr/dot_general | solution.py:35
  57.1 2.1 %fusion.74 = (f32[4]{0:T(128)S(1)}, f32[4,1024]{1,0:T(4,128)S(1)}) fusion(bf16[1024,1024]{1,0:T(8,128)(2,1)} %get-tuple-element.914, f32[4,1024]{1,0:T(4,128)S(1)} %get-tuple-element.902, pred[]{:T(512)S(6)} %compare.6, f32[1024]{0:T(1024)S(1)} %get-tuple-element.913, pred[4]{0:T(512)(128)(4,1)S(1)} %compare_bitcast_fusion.16, ...), kind=kOutput, calls=%fused_computation.70.clone.1 | convolution fusion | flops 8404988 | bytes 2150425 | tf_op jit(solution)/shard_map/while/body/eval_jaxpr/dot_general | solution.py:35
  59.3 2.1 %fusion.74 = (f32[4]{0:T(128)S(1)}, f32[4,1024]{1,0:T(4,128)S(1)}) fusion(bf16[1024,1024]{1,0:T(8,128)(2,1)} %get-tuple-element.914, f32[4,1024]{1,0:T(4,128)S(1)} %get-tuple-element.902, pred[]{:T(512)S(6)} %compare.6, f32[1024]{0:T(1024)S(1)} %get-tuple-element.913, pred[4]{0:T(512)(128)(4,1)S(1)} %compare_bitcast_fusion.16, ...), kind=kOutput, calls=%fused_computation.70.clone.1 | convolution fusion | flops 8404988 | bytes 2150425 | tf_op jit(solution)/shard_map/while/body/eval_jaxpr/dot_general | solution.py:35
  61.5 2.1 %fusion.74 = (f32[4]{0:T(128)S(1)}, f32[4,1024]{1,0:T(4,128)S(1)}) fusion(bf16[1024,1024]{1,0:T(8,128)(2,1)} %get-tuple-element.914, f32[4,1024]{1,0:T(4,128)S(1)} %get-tuple-element.902, pred[]{:T(512)S(6)} %compare.6, f32[1024]{0:T(1024)S(1)} %get-tuple-element.913, pred[4]{0:T(512)(128)(4,1)S(1)} %compare_bitcast_fusion.16, ...), kind=kOutput, calls=%fused_computation.70.clone.1 | convolution fusion | flops 8404988 | bytes 2150425 | tf_op jit(solution)/shard_map/while/body/eval_jaxpr/dot_general | solution.py:35
  63.7 5.2 %collective-permute-start = (f32[4,1024]{1,0:T(4,128)S(1)}, f32[4,1024]{1,0:T(4,128)S(1)}, u32[]{:S(2)}, u32[]{:S(2)}) collective-permute-start(f32[4,1024]{1,0:T(4,128)S(1)} %get-tuple-element.437), channel_id=1, source_target_pairs={{0,1},{1,2},{2,3},{3,4},{4,5},{5,6},{6,7},{7,8},{8,9},{9,10},{10,1... | collective-permute-start | bytes 49160 | tf_op jit(solution)/shard_map/ppermute | solution.py:15
  69.0 4.8 %while.82 = (s32[]{:T(128)}, f32[4,1024]{1,0:T(4,128)S(1)}, s32[8,4]{1,0:T(8,128)S(1)}, f32[8,4,1024]{2,1,0:T(4,128)S(1)}, bf16[1024,1024]{1,0:T(8,128)(2,1)S(1)}, /*index=5*/s32[]{:T(128)}, s32[]{:T(128)}) while((s32[]{:T(128)}, f32[4,1024]{1,0:T(4,128)S(1)}, s32[8,4]{1,0:T(8,128)S(1)}, f32[8,4,1024]{2,1,0:T(4,128)S(1)}, ...), condition=%wide.region_17.18_spmd, body=%wide.region_15.17_spmd.sunk | while | flops 8409091 | bytes 2179225 | solution.py:57
  69.0 0.5 fusion.70
  69.6 0.5 fusion.70
  70.2 0.5 fusion.70
  71.4 0.5 fusion.70
  73.2 0.5 fusion.70
  73.8 1.9 %collective-permute-start.3 = (f32[4,1024]{1,0:T(4,128)S(1)}, f32[4,1024]{1,0:T(4,128)S(1)}, u32[]{:S(2)}, u32[]{:S(2)}) collective-permute-start(f32[4,1024]{1,0:T(4,128)S(1)} %get-tuple-element.441), channel_id=1, source_target_pairs={{1,0},{2,1},{3,2},{4,3},{5,4},{6,5},{7,6},{8,7},{9,8},{10,9},{11,1... | collective-permute-start | bytes 49160 | tf_op jit(solution)/shard_map/ppermute | solution.py:15
  75.7 17.6 %while.80 = (s32[]{:T(128)}, f32[4,1024]{1,0:T(4,128)S(1)}, f32[8,4,1024]{2,1,0:T(4,128)S(1)}, s32[8,4]{1,0:T(8,128)S(1)}, f32[1024]{0:T(1024)S(1)}, /*index=5*/bf16[1024,1024]{1,0:T(8,128)(2,1)}, s32[]{:T(128)}) while((s32[]{:T(128)}, f32[4,1024]{1,0:T(4,128)S(1)}, f32[8,4,1024]{2,1,0:T(4,128)S(1)}, s32[8,4]{1,0:T(8,128)S(1)}, ...), condition=%wide.region_8.9_spmd, body=%wide.region_6.8_spmd.sunk | while | flops 8409090 | bytes 2183317 | solution.py:44
  75.7 2.1 %fusion.65 = (f32[4]{0:T(128)S(1)}, f32[4,1024]{1,0:T(4,128)S(1)}) fusion(bf16[1024,1024]{1,0:T(8,128)(2,1)} %get-tuple-element.936, f32[4,1024]{1,0:T(4,128)S(1)} %get-tuple-element.925, f32[1024]{0:T(1024)S(1)} %get-tuple-element.935, pred[4]{0:T(512)(128)(4,1)S(1)} %compare_bitcast_fusion.12, f32[8,4,1024]{2,1,0:T(4,128)S(1)} %get-tuple-element.933, ...), kind=kOutput, calls=%fused_computation.66.clone.1 | convolution fusion | flops 8404988 | bytes 2150424 | tf_op jit(solution)/shard_map/while/body/eval_jaxpr/dot_general | solution.py:35
  77.9 2.1 %fusion.65 = (f32[4]{0:T(128)S(1)}, f32[4,1024]{1,0:T(4,128)S(1)}) fusion(bf16[1024,1024]{1,0:T(8,128)(2,1)} %get-tuple-element.936, f32[4,1024]{1,0:T(4,128)S(1)} %get-tuple-element.925, f32[1024]{0:T(1024)S(1)} %get-tuple-element.935, pred[4]{0:T(512)(128)(4,1)S(1)} %compare_bitcast_fusion.12, f32[8,4,1024]{2,1,0:T(4,128)S(1)} %get-tuple-element.933, ...), kind=kOutput, calls=%fused_computation.66.clone.1 | convolution fusion | flops 8404988 | bytes 2150424 | tf_op jit(solution)/shard_map/while/body/eval_jaxpr/dot_general | solution.py:35
  80.1 2.1 %fusion.65 = (f32[4]{0:T(128)S(1)}, f32[4,1024]{1,0:T(4,128)S(1)}) fusion(bf16[1024,1024]{1,0:T(8,128)(2,1)} %get-tuple-element.936, f32[4,1024]{1,0:T(4,128)S(1)} %get-tuple-element.925, f32[1024]{0:T(1024)S(1)} %get-tuple-element.935, pred[4]{0:T(512)(128)(4,1)S(1)} %compare_bitcast_fusion.12, f32[8,4,1024]{2,1,0:T(4,128)S(1)} %get-tuple-element.933, ...), kind=kOutput, calls=%fused_computation.66.clone.1 | convolution fusion | flops 8404988 | bytes 2150424 | tf_op jit(solution)/shard_map/while/body/eval_jaxpr/dot_general | solution.py:35
  82.3 2.1 %fusion.65 = (f32[4]{0:T(128)S(1)}, f32[4,1024]{1,0:T(4,128)S(1)}) fusion(bf16[1024,1024]{1,0:T(8,128)(2,1)} %get-tuple-element.936, f32[4,1024]{1,0:T(4,128)S(1)} %get-tuple-element.925, f32[1024]{0:T(1024)S(1)} %get-tuple-element.935, pred[4]{0:T(512)(128)(4,1)S(1)} %compare_bitcast_fusion.12, f32[8,4,1024]{2,1,0:T(4,128)S(1)} %get-tuple-element.933, ...), kind=kOutput, calls=%fused_computation.66.clone.1 | convolution fusion | flops 8404988 | bytes 2150424 | tf_op jit(solution)/shard_map/while/body/eval_jaxpr/dot_general | solution.py:35
  84.5 2.1 %fusion.65 = (f32[4]{0:T(128)S(1)}, f32[4,1024]{1,0:T(4,128)S(1)}) fusion(bf16[1024,1024]{1,0:T(8,128)(2,1)} %get-tuple-element.936, f32[4,1024]{1,0:T(4,128)S(1)} %get-tuple-element.925, f32[1024]{0:T(1024)S(1)} %get-tuple-element.935, pred[4]{0:T(512)(128)(4,1)S(1)} %compare_bitcast_fusion.12, f32[8,4,1024]{2,1,0:T(4,128)S(1)} %get-tuple-element.933, ...), kind=kOutput, calls=%fused_computation.66.clone.1 | convolution fusion | flops 8404988 | bytes 2150424 | tf_op jit(solution)/shard_map/while/body/eval_jaxpr/dot_general | solution.py:35
  86.7 2.1 %fusion.65 = (f32[4]{0:T(128)S(1)}, f32[4,1024]{1,0:T(4,128)S(1)}) fusion(bf16[1024,1024]{1,0:T(8,128)(2,1)} %get-tuple-element.936, f32[4,1024]{1,0:T(4,128)S(1)} %get-tuple-element.925, f32[1024]{0:T(1024)S(1)} %get-tuple-element.935, pred[4]{0:T(512)(128)(4,1)S(1)} %compare_bitcast_fusion.12, f32[8,4,1024]{2,1,0:T(4,128)S(1)} %get-tuple-element.933, ...), kind=kOutput, calls=%fused_computation.66.clone.1 | convolution fusion | flops 8404988 | bytes 2150424 | tf_op jit(solution)/shard_map/while/body/eval_jaxpr/dot_general | solution.py:35
  88.9 2.1 %fusion.65 = (f32[4]{0:T(128)S(1)}, f32[4,1024]{1,0:T(4,128)S(1)}) fusion(bf16[1024,1024]{1,0:T(8,128)(2,1)} %get-tuple-element.936, f32[4,1024]{1,0:T(4,128)S(1)} %get-tuple-element.925, f32[1024]{0:T(1024)S(1)} %get-tuple-element.935, pred[4]{0:T(512)(128)(4,1)S(1)} %compare_bitcast_fusion.12, f32[8,4,1024]{2,1,0:T(4,128)S(1)} %get-tuple-element.933, ...), kind=kOutput, calls=%fused_computation.66.clone.1 | convolution fusion | flops 8404988 | bytes 2150424 | tf_op jit(solution)/shard_map/while/body/eval_jaxpr/dot_general | solution.py:35
  91.1 2.1 %fusion.65 = (f32[4]{0:T(128)S(1)}, f32[4,1024]{1,0:T(4,128)S(1)}) fusion(bf16[1024,1024]{1,0:T(8,128)(2,1)} %get-tuple-element.936, f32[4,1024]{1,0:T(4,128)S(1)} %get-tuple-element.925, f32[1024]{0:T(1024)S(1)} %get-tuple-element.935, pred[4]{0:T(512)(128)(4,1)S(1)} %compare_bitcast_fusion.12, f32[8,4,1024]{2,1,0:T(4,128)S(1)} %get-tuple-element.933, ...), kind=kOutput, calls=%fused_computation.66.clone.1 | convolution fusion | flops 8404988 | bytes 2150424 | tf_op jit(solution)/shard_map/while/body/eval_jaxpr/dot_general | solution.py:35
  93.3 5.4 %collective-permute-start.1 = (f32[4,1024]{1,0:T(4,128)S(1)}, f32[4,1024]{1,0:T(4,128)S(1)}, u32[]{:S(2)}, u32[]{:S(2)}) collective-permute-start(f32[4,1024]{1,0:T(4,128)S(1)} %get-tuple-element.438), channel_id=1, source_target_pairs={{0,1},{1,2},{2,3},{3,4},{4,5},{5,6},{6,7},{7,8},{8,9},{9,10},{10,1... | collective-permute-start | bytes 49160 | tf_op jit(solution)/shard_map/ppermute | solution.py:15
  98.8 6.3 %while.83 = (s32[]{:T(128)}, f32[4,1024]{1,0:T(4,128)S(1)}, f32[8,4,1024]{2,0,1:T(8,128)S(1)}, s32[8,4]{1,0:T(8,128)S(1)}, f32[8,4,1024]{2,1,0:T(4,128)S(1)}, /*...) while((s32[]{:T(128)}, f32[4,1024]{1,0:T(4,128)S(1)}, ...), condition=%wide.region_20.21_spmd, body=%wide.region_18.20_spmd.sunk | while | flops 8409091 | bytes 2244781 | solution.py:57
  105.1 20.1 %while.81 = (s32[]{:T(128)}, f32[4,1024]{1,0:T(4,128)S(1)}, f32[8,4,1024]{2,0,1:T(8,128)S(1)}, f32[8,4]{1,0:T(8,128)S(1)}, f32[8,4,1024]{2,1,0:T(4,128)S(1)}, /*...) while((s32[]{:T(128)}, f32[4,1024]{1,0:T(4,128)S(1)}, ...), condition=%wide.region_11.12_spmd, body=%wide.region_9.11_spmd.sunk | while | flops 8413186 | bytes 2281733 | solution.py:44
  105.1 2.1 %fusion.67 = (f32[4]{0:T(128)S(1)}, f32[4,1024]{1,0:T(4,128)S(1)}) fusion(bf16[1024,1024]{1,0:T(8,128)(2,1)} %get-tuple-element.965, f32[4,1024]{1,0:T(4,128)S(1)} %get-tuple-element.949, f32[1024]{0:T(1024)S(1)} %get-tuple-element.964, pred[4]{0:T(512)(128)(4,1)S(1)} %compare_bitcast_fusion.13, f32[8,4,1024]{2,1,0:T(4,128)S(1)} %get-tuple-element.962, ...), kind=kOutput, calls=%fused_computation.67.clone.1 | convolution fusion | flops 8404988 | bytes 2150424 | tf_op jit(solution)/shard_map/while/body/eval_jaxpr/dot_general | solution.py:35
  107.6 2.1 %fusion.67 = (f32[4]{0:T(128)S(1)}, f32[4,1024]{1,0:T(4,128)S(1)}) fusion(bf16[1024,1024]{1,0:T(8,128)(2,1)} %get-tuple-element.965, f32[4,1024]{1,0:T(4,128)S(1)} %get-tuple-element.949, f32[1024]{0:T(1024)S(1)} %get-tuple-element.964, pred[4]{0:T(512)(128)(4,1)S(1)} %compare_bitcast_fusion.13, f32[8,4,1024]{2,1,0:T(4,128)S(1)} %get-tuple-element.962, ...), kind=kOutput, calls=%fused_computation.67.clone.1 | convolution fusion | flops 8404988 | bytes 2150424 | tf_op jit(solution)/shard_map/while/body/eval_jaxpr/dot_general | solution.py:35
  110.1 2.1 %fusion.67 = (f32[4]{0:T(128)S(1)}, f32[4,1024]{1,0:T(4,128)S(1)}) fusion(bf16[1024,1024]{1,0:T(8,128)(2,1)} %get-tuple-element.965, f32[4,1024]{1,0:T(4,128)S(1)} %get-tuple-element.949, f32[1024]{0:T(1024)S(1)} %get-tuple-element.964, pred[4]{0:T(512)(128)(4,1)S(1)} %compare_bitcast_fusion.13, f32[8,4,1024]{2,1,0:T(4,128)S(1)} %get-tuple-element.962, ...), kind=kOutput, calls=%fused_computation.67.clone.1 | convolution fusion | flops 8404988 | bytes 2150424 | tf_op jit(solution)/shard_map/while/body/eval_jaxpr/dot_general | solution.py:35
  112.7 2.1 %fusion.67 = (f32[4]{0:T(128)S(1)}, f32[4,1024]{1,0:T(4,128)S(1)}) fusion(bf16[1024,1024]{1,0:T(8,128)(2,1)} %get-tuple-element.965, f32[4,1024]{1,0:T(4,128)S(1)} %get-tuple-element.949, f32[1024]{0:T(1024)S(1)} %get-tuple-element.964, pred[4]{0:T(512)(128)(4,1)S(1)} %compare_bitcast_fusion.13, f32[8,4,1024]{2,1,0:T(4,128)S(1)} %get-tuple-element.962, ...), kind=kOutput, calls=%fused_computation.67.clone.1 | convolution fusion | flops 8404988 | bytes 2150424 | tf_op jit(solution)/shard_map/while/body/eval_jaxpr/dot_general | solution.py:35
  115.2 2.1 %fusion.67 = (f32[4]{0:T(128)S(1)}, f32[4,1024]{1,0:T(4,128)S(1)}) fusion(bf16[1024,1024]{1,0:T(8,128)(2,1)} %get-tuple-element.965, f32[4,1024]{1,0:T(4,128)S(1)} %get-tuple-element.949, f32[1024]{0:T(1024)S(1)} %get-tuple-element.964, pred[4]{0:T(512)(128)(4,1)S(1)} %compare_bitcast_fusion.13, f32[8,4,1024]{2,1,0:T(4,128)S(1)} %get-tuple-element.962, ...), kind=kOutput, calls=%fused_computation.67.clone.1 | convolution fusion | flops 8404988 | bytes 2150424 | tf_op jit(solution)/shard_map/while/body/eval_jaxpr/dot_general | solution.py:35
  117.7 2.1 %fusion.67 = (f32[4]{0:T(128)S(1)}, f32[4,1024]{1,0:T(4,128)S(1)}) fusion(bf16[1024,1024]{1,0:T(8,128)(2,1)} %get-tuple-element.965, f32[4,1024]{1,0:T(4,128)S(1)} %get-tuple-element.949, f32[1024]{0:T(1024)S(1)} %get-tuple-element.964, pred[4]{0:T(512)(128)(4,1)S(1)} %compare_bitcast_fusion.13, f32[8,4,1024]{2,1,0:T(4,128)S(1)} %get-tuple-element.962, ...), kind=kOutput, calls=%fused_computation.67.clone.1 | convolution fusion | flops 8404988 | bytes 2150424 | tf_op jit(solution)/shard_map/while/body/eval_jaxpr/dot_general | solution.py:35
  120.2 2.1 %fusion.67 = (f32[4]{0:T(128)S(1)}, f32[4,1024]{1,0:T(4,128)S(1)}) fusion(bf16[1024,1024]{1,0:T(8,128)(2,1)} %get-tuple-element.965, f32[4,1024]{1,0:T(4,128)S(1)} %get-tuple-element.949, f32[1024]{0:T(1024)S(1)} %get-tuple-element.964, pred[4]{0:T(512)(128)(4,1)S(1)} %compare_bitcast_fusion.13, f32[8,4,1024]{2,1,0:T(4,128)S(1)} %get-tuple-element.962, ...), kind=kOutput, calls=%fused_computation.67.clone.1 | convolution fusion | flops 8404988 | bytes 2150424 | tf_op jit(solution)/shard_map/while/body/eval_jaxpr/dot_general | solution.py:35
  122.7 2.1 %fusion.67 = (f32[4]{0:T(128)S(1)}, f32[4,1024]{1,0:T(4,128)S(1)}) fusion(bf16[1024,1024]{1,0:T(8,128)(2,1)} %get-tuple-element.965, f32[4,1024]{1,0:T(4,128)S(1)} %get-tuple-element.949, f32[1024]{0:T(1024)S(1)} %get-tuple-element.964, pred[4]{0:T(512)(128)(4,1)S(1)} %compare_bitcast_fusion.13, f32[8,4,1024]{2,1,0:T(4,128)S(1)} %get-tuple-element.962, ...), kind=kOutput, calls=%fused_computation.67.clone.1 | convolution fusion | flops 8404988 | bytes 2150424 | tf_op jit(solution)/shard_map/while/body/eval_jaxpr/dot_general | solution.py:35
  125.2 0.7 copy.49
  125.9 0.7 copy.47
  126.6 1.1 reshape.117
  127.8 3.4 %all_to_all.36 = bf16[2,2,8192]{2,1,0:T(2,128)(2,1)S(1)} all-to-all(bf16[2,2,8192]{2,1,0:T(2,128)(2,1)S(1)} %reshape.117), channel_id=1, replica_groups=mesh['tm'=16,'state'=2] {'state'}, dimensions={0} | all-to-all | bytes 131072 | tf_op jit(solution)/shard_map/all_to_all | solution.py:107
  131.2 1.2 reshape.118
  132.4 1.2 copy.48
  (197 shorter events, 14.4 us)
Async XLA Ops:
  7.2 10.4 %copy-start = (s32[4,16]{1,0:T(4,128)S(1)}, s32[4,16]{1,0:T(4,128)}, u32[]{:S(2)}) copy-start(s32[4,16]{1,0:T(4,128)} %param.23) | copy-start | bytes 772
  7.2 2.5 %copy-start.2 = (f32[512,512]{1,0:T(8,128)S(1)}, f32[512,512]{1,0:T(8,128)}, u32[]{:S(2)}) copy-start(f32[512,512]{1,0:T(8,128)} %param.20) | copy-start | bytes 3145732
  7.2 2.5 %copy-start.3 = (f32[512,512]{1,0:T(8,128)S(1)}, f32[512,512]{1,0:T(8,128)}, u32[]{:S(2)}) copy-start(f32[512,512]{1,0:T(8,128)} %param.19) | copy-start | bytes 3145732
  7.2 15.1 %all-gather.3.cloned.1.call-start = ((), (), s32[]{:S(2)}) async-start(), calls=%async_computation.2 | async-start | bytes 3145728 | tf_op jit(solution)/shard_map/all_gather | solution.py:81
  9.7 0.9 copy-start.4
  10.6 7.2 %copy-start.5 = (bf16[512]{0:T(512)(128)(2,1)S(1)}, bf16[512]{0:T(512)(128)(2,1)}, u32[]{:S(2)}) copy-start(bf16[512]{0:T(512)(128)(2,1)} %param.22) | copy-start | bytes 3076
  13.6 5.2 %all-to-all-start = ((f32[4,16,512]{2,0,1:T(4,128)}), f32[4,16,512]{2,0,1:T(4,128)S(1)}, u32[]{:S(2)}, u32[]{:S(2)}) async-start(f32[4,16,512]{2,0,1:T(4,128)} %copy.38), calls=%async_computation | async-start | bytes 262144 | tf_op jit(solution)/shard_map/all_to_all | solution.py:102
  39.9 29.0 %collective-permute-start.2 = (f32[4,1024]{1,0:T(4,128)S(1)}, f32[4,1024]{1,0:T(4,128)S(1)}, u32[]{:S(2)}, u32[]{:S(2)}) collective-permute-start(f32[4,1024]{1,0:T(4,128)S(1)} %get-tuple-element.440), channel_id=1, source_target_pairs={{1,0},{2,1},{3,2},{4,3},{5,4},{6,5},{7,6},{8,7},{9,8},{10,9},{11,1... | collective-permute-start | bytes 49160 | tf_op jit(solution)/shard_map/ppermute | solution.py:15
  46.0 23.0 %copy-start.1 = (bf16[1024,1024]{1,0:T(8,128)(2,1)S(1)}, bf16[1024,1024]{1,0:T(8,128)(2,1)}, u32[]{:S(2)}) copy-start(bf16[1024,1024]{1,0:T(8,128)(2,1)} %get-tuple-element.1042) | copy-start | bytes 6291460
  63.7 12.0 %collective-permute-start = (f32[4,1024]{1,0:T(4,128)S(1)}, f32[4,1024]{1,0:T(4,128)S(1)}, u32[]{:S(2)}, u32[]{:S(2)}) collective-permute-start(f32[4,1024]{1,0:T(4,128)S(1)} %get-tuple-element.437), channel_id=1, source_target_pairs={{0,1},{1,2},{2,3},{3,4},{4,5},{5,6},{6,7},{7,8},{8,9},{9,10},{10,1... | collective-permute-start | bytes 49160 | tf_op jit(solution)/shard_map/ppermute | solution.py:15
  73.8 25.0 %collective-permute-start.3 = (f32[4,1024]{1,0:T(4,128)S(1)}, f32[4,1024]{1,0:T(4,128)S(1)}, u32[]{:S(2)}, u32[]{:S(2)}) collective-permute-start(f32[4,1024]{1,0:T(4,128)S(1)} %get-tuple-element.441), channel_id=1, source_target_pairs={{1,0},{2,1},{3,2},{4,3},{5,4},{6,5},{7,6},{8,7},{9,8},{10,9},{11,1... | collective-permute-start | bytes 49160 | tf_op jit(solution)/shard_map/ppermute | solution.py:15
  93.3 11.8 %collective-permute-start.1 = (f32[4,1024]{1,0:T(4,128)S(1)}, f32[4,1024]{1,0:T(4,128)S(1)}, u32[]{:S(2)}, u32[]{:S(2)}) collective-permute-start(f32[4,1024]{1,0:T(4,128)S(1)} %get-tuple-element.438), channel_id=1, source_target_pairs={{0,1},{1,2},{2,3},{3,4},{4,5},{5,6},{6,7},{7,8},{8,9},{9,10},{10,1... | collective-permute-start | bytes 49160 | tf_op jit(solution)/shard_map/ppermute | solution.py:15
Sparse Core Ops, SparseCore 0:
  9.8 12.4 all-gather.2
where the time goes:
time: 142 us; the launch traced here: 140 us
  matrix products  77.4 us (55%)
  starting transfers between devices  18.8 us (13%)
  local copies, waits for them, and re-layouts  15.8 us (11%)
  between operations  14.2 us (10%)
  other arithmetic  6.92 us (5%)
  blocking collectives  5.28 us (4%)
    dot_general x24, matrix products, forward_step(): jnp.dot(alpha_prev.astype(jnp.bfloat16), trans, preferred_element_type=jn...  50.5 us
    dot_general x24, matrix products, backward_step(): jnp.dot((emit_row * beta_next).astype(jnp.bfloat16), trans_back, preferre...  24.7 us
    ppermute x4, starting transfers between devices, passed_along(): return lax.ppermute(block, axis, route)  14.7 us
    unnamed x18, local copies, waits for them, and re-layouts  9.42 us
    all_to_all x1, starting transfers between devices, per_device(): lax.all_to_all(scores, 'state', split_axis=1, concat_axis=2, tiled=True)  4.04 us
    all_to_all x1, blocking collectives, per_device(): lax.all_to_all(posterior, 'state', split_axis=2, concat_axis=1, tiled=True)  3.45 us
    dynamic_update_slice x40, local copies, waits for them, and re-layouts, run_block(): lax.scan(forward_step, alpha_in, (emission_t, reset_t))  2.92 us
  transfers between devices with their start and end apart: 6, of which 2 were waited for; matrix products, arithmetic and copies ran while one was open for 39% of the time, Pallas kernels for 0%

commit v1 on v0

v1 whole, which is shorter than its diff:
```python
import functools

import jax
import jax.numpy as jnp
from jax import lax
from jax.experimental import pallas as pl
from jax.experimental.pallas import tpu as pltpu
from jax.sharding import PartitionSpec as P

MAXLEN = 16
ACOUSTIC = 0.1
MESH = pl.DeviceIdType.MESH
F32 = jnp.float32
BF16 = jnp.bfloat16
PAD = 8
LANES = 128


def split(a):
    hi = a.astype(BF16)
    return hi, (a - hi.astype(F32)).astype(BF16)


def dot_t(a, b):
    return lax.dot_general(a, b, (((1,), (1,)), ((), ())), preferred_element_type=F32)


def kernel(
    blocks, feat, means, prec, trans, init, flags, post, evid,
    xin, raw, wt, prior_in, w_hi, w_lo, sc, sc_in, em, xb, y, inv, flag_pad, mask, fin, fin_in,
    send, recv,
):
    c = lax.axis_index("tm")
    s = lax.axis_index("state")
    o = 1 - s
    nxt = lax.rem(c + 1, blocks)
    prv = lax.rem(c + blocks - 1, blocks)
    streams, frames, width = feat.shape
    half = trans.shape[0]
    states = trans.shape[1]
    rows = streams * frames
    chunk = min(256, states)

    barrier = pltpu.get_barrier_semaphore()
    for who in ((nxt, s), (prv, s), (c, o)):
        pl.semaphore_signal(barrier, inc=1, device_id=who, device_id_type=MESH)

    row_t = lax.broadcasted_iota(jnp.int32, (frames, frames), 0)
    col_t = lax.broadcasted_iota(jnp.int32, (frames, frames), 1)
    for b in range(streams):
        at = rows + b * frames
        xin[at : at + frames, :width] = feat[b]
        line = jnp.broadcast_to(flags[b : b + 1, :].astype(F32), (frames, frames))
        column = jnp.sum(jnp.where(row_t == col_t, line, 0.0), axis=1, keepdims=True)
        xin[at : at + frames, width:] = jnp.broadcast_to(column, (frames, LANES))
    mine = pl.ds(pl.multiple_of(s * half, half), half)
    theirs = pl.ds(pl.multiple_of(o * half, half), half)
    prior_in[:, mine] = jnp.broadcast_to(init[...].astype(F32), (8, half))

    pl.semaphore_wait(barrier, 3)

    def remote(src, dst, k, who):
        return pltpu.make_async_remote_copy(
            src_ref=src, dst_ref=dst, send_sem=send.at[k], recv_sem=recv.at[k],
            device_id=who, device_id_type=MESH,
        )

    own = xin.at[pl.ds(rows, rows)]
    to_next = remote(own, xin.at[pl.ds(0, rows)], 0, (nxt, s))
    to_prev = remote(own, xin.at[pl.ds(2 * rows, rows)], 1, (prv, s))
    trans_copy = remote(trans, raw.at[mine], 2, (c, o))
    prior_copy = remote(prior_in.at[:, mine], prior_in.at[:, mine], 3, (c, o))
    to_next.start()
    to_prev.start()
    trans_copy.start()
    prior_copy.start()

    p = prec[...]
    m = means[...]
    pm = p * m
    hi, lo = split(-0.5 * p)
    w_hi[:, :width] = hi
    w_lo[:, :width] = lo
    hi, lo = split(pm)
    w_hi[:, width:] = hi
    w_lo[:, width:] = lo
    offset = 0.5 * jnp.sum(jnp.log(p) - pm * m, axis=1, keepdims=True)
    offset = jnp.broadcast_to(offset, (half, LANES)).T[0:1]
    raw[mine, :] = trans[...]

    @pl.when(s == 1)
    def _():
        wt[:, half:] = trans[...].T

    to_next.wait_recv()
    to_prev.wait_recv()
    x = xin[:, :width]
    sq_hi, sq_lo = split(x * x)
    x_hi, x_lo = split(x)
    left_hi = jnp.concatenate([sq_hi, x_hi], axis=1)
    left_lo = jnp.concatenate([sq_lo, x_lo], axis=1)
    total = dot_t(left_hi, w_hi[...]) + (dot_t(left_lo, w_hi[...]) + dot_t(left_hi, w_lo[...]))
    sc[...] = ACOUSTIC * (total + offset)

    window = pl.ds(pl.multiple_of(s * rows, rows), 2 * rows)
    other_window = pl.ds(pl.multiple_of(o * rows, rows), 2 * rows)
    score_copy = remote(sc.at[other_window], sc_in, 4, (c, o))
    score_copy.start()

    trans_copy.wait_recv()
    prior_copy.wait_recv()

    @pl.when(s == 1)
    def _():
        wt[:, :half] = raw[:half, :].T

    flag_pad[...] = jnp.ones_like(flag_pad)
    y[:, :PAD] = jnp.ones((streams, PAD, states), F32)
    y[:, PAD + 2 * frames :] = jnp.ones((streams, PAD, states), F32)
    for h in range(2):
        for b in range(streams):
            at = pl.multiple_of((s + h) * rows + b * frames, frames)
            flag_pad[b, PAD + h * frames : PAD + (h + 1) * frames] = xin[pl.ds(at, frames), width:]

    score_copy.wait_recv()
    for i in range(0, 2 * rows, 32):
        at = pl.multiple_of(s * rows + i, 32)
        a = sc[pl.ds(at, 32)]
        z = sc_in[i : i + 32]
        top = jnp.maximum(jnp.max(a, axis=1, keepdims=True), jnp.max(z, axis=1, keepdims=True))
        em[i : i + 32, mine] = jnp.exp(a - top)
        em[i : i + 32, theirs] = jnp.exp(z - top)

    pieces = [(h, b, (h * streams + b) * frames) for h in range(2) for b in range(streams)]

    def spread(a):
        return jnp.concatenate([a] * (chunk // LANES), axis=1)

    def chain(weights, forward):
        d = -1 if forward else 1
        held = 1 if forward else 0
        if forward:
            prior = prior_in[...]
            prior = prior / jnp.sum(prior, axis=1, keepdims=True)
        else:
            prior = jnp.full((8, states), 1.0 / states, F32)
        base = prior[0:1]

        for h, b, r in pieces:
            first = PAD + h * frames + (0 if forward else 1)
            mask[r : r + frames] = flag_pad[b, first : first + frames]
            x0 = em[r : r + frames] * base
            xb[0, r : r + frames] = x0.astype(BF16)
            inv[r : r + frames] = jnp.broadcast_to(
                1.0 / jnp.sum(x0, axis=1, keepdims=True), (frames, LANES)
            )

        def step(now, later, last):
            sums = [None] * len(pieces)
            for n in range(0, states, chunk):
                cols = slice(n, n + chunk)
                out = jnp.dot(xb[now], weights[:, cols], preferred_element_type=F32)
                for h, b, r in pieces:
                    at = PAD + h * frames
                    y[b, at : at + frames, cols] = out[r : r + frames] * spread(inv[r : r + frames])
                for k, (h, b, r) in enumerate(pieces):
                    if last and h != held:
                        continue
                    at = PAD + h * frames + d
                    reset = spread(mask[r : r + frames]) > 0.5
                    value = jnp.where(reset, base[:, cols], y[b, at : at + frames, cols])
                    if last and not forward:
                        fin[b * frames : (b + 1) * frames, cols] = value
                        continue
                    value = em[r : r + frames, cols] * value
                    if last:
                        fin[b * frames : (b + 1) * frames, cols] = value
                    else:
                        xb[later, r : r + frames, cols] = value.astype(BF16)
                    part = sum(value[:, i : i + LANES] for i in range(0, chunk, LANES))
                    sums[k] = part if sums[k] is None else sums[k] + part
            for k, (h, b, r) in enumerate(pieces):
                if sums[k] is None:
                    continue
                norm = jnp.sum(sums[k], axis=1, keepdims=True)
                if last:
                    at = b * frames
                    fin[at : at + frames, :states] = fin[at : at + frames, :states] / norm
                    fin[at : at + frames, states:] = jnp.broadcast_to(jnp.log(norm), (frames, LANES))
                else:
                    inv[r : r + frames] = jnp.broadcast_to(1.0 / norm, (frames, LANES))

        def two(i, carry):
            step(0, 1, False)
            step(1, 0, False)
            return carry

        turns = MAXLEN - 2
        lax.fori_loop(0, turns // 2, two, 0)
        if turns % 2:
            step(0, 1, False)
        step(turns % 2, 1 - turns % 2, True)
        if not forward:
            fin[:, states:] = jnp.zeros((rows, LANES), F32)

    @pl.when(s == 0)
    def _():
        chain(raw, True)

    @pl.when(s == 1)
    def _():
        chain(wt, False)

    fin_copy = remote(fin, fin_in, 5, (c, o))
    fin_copy.start()
    fin_copy.wait_recv()
    for b in range(streams):
        at = b * frames
        rows_b = slice(at, at + frames)
        product = fin[rows_b, :states] * fin_in[rows_b, :states]
        scale = 1.0 / jnp.sum(product, axis=1, keepdims=True)
        post[b] = (fin[rows_b, mine] * fin_in[rows_b, mine] * scale).astype(BF16)

    part = frames // 2
    row_e = lax.broadcasted_iota(jnp.int32, (part, LANES), 0)
    col_e = lax.broadcasted_iota(jnp.int32, (part, LANES), 1)
    for b in range(streams):
        at = pl.ds(pl.multiple_of(b * frames + s * part, part), part)
        logs = fin[at, states:] + fin_in[at, states:]
        line = jnp.sum(jnp.where(row_e == col_e, logs, 0.0), axis=0, keepdims=True)
        evid[b : b + 1, :] = line[:, :part]

    for copy in (to_next, to_prev, trans_copy, prior_copy, score_copy, fin_copy):
        copy.wait_send()


def per_device(features, gauss_means, precisions, transitions, initial, reset_flags):
    streams, frames, width = features.shape
    half, states = transitions.shape
    rows = streams * frames
    blocks = lax.axis_size("tm")
    vmem = pl.BlockSpec(memory_space=pltpu.VMEM)
    return pl.pallas_call(
        functools.partial(kernel, blocks),
        out_shape=(
            jax.ShapeDtypeStruct((streams, frames, half), BF16),
            jax.ShapeDtypeStruct((streams, frames // 2), F32),
        ),
        in_specs=[vmem] * 6,
        out_specs=(vmem, vmem),
        scratch_shapes=[
            pltpu.VMEM((3 * rows, width + LANES), F32),
            pltpu.VMEM((states, states), BF16),
            pltpu.VMEM((states, states), BF16),
            pltpu.VMEM((8, states), F32),
            pltpu.VMEM((half, 2 * width), BF16),
            pltpu.VMEM((half, 2 * width), BF16),
            pltpu.VMEM((3 * rows, half), F32),
            pltpu.VMEM((2 * rows, half), F32),
            pltpu.VMEM((2 * rows, states), F32),
            pltpu.VMEM((2, 2 * rows, states), BF16),
            pltpu.VMEM((streams, 2 * frames + 2 * PAD, states), F32),
            pltpu.VMEM((2 * rows, LANES), F32),
            pltpu.VMEM((streams, 2 * frames + 2 * PAD, LANES), F32),
            pltpu.VMEM((2 * rows, LANES), F32),
            pltpu.VMEM((rows, states + LANES), F32),
            pltpu.VMEM((rows, states + LANES), F32),
            pltpu.SemaphoreType.DMA((6,)),
            pltpu.SemaphoreType.DMA((6,)),
        ],
        compiler_params=pltpu.CompilerParams(
            collective_id=0, has_side_effects=True, vmem_limit_bytes=40 * 1024 * 1024
        ),
    )(features, gauss_means, precisions, transitions, initial.reshape(1, half), reset_flags)


def solution(mesh):
    return jax.shard_map(
        per_device,
        mesh=mesh,
        in_specs=(
            P(None, "tm", None),
            P("state", None),
            P("state", None),
            P("state", None),
            P("state"),
            P(None, "tm"),
        ),
        out_specs=(P(None, "tm", "state"), P(None, ("tm", "state"))),
        check_vma=False,
    )
```

time: 142 us -> 31.1 us (0.22)
  the two profiles are of different devices: /device:TPU:7 before, /device:TPU:0 now
where the time goes in v1:
time: 31.1 us; the launch traced here: 30.8 us
  Pallas kernels  23.7 us (76%)
  local copies, waits for them, and re-layouts  6.48 us (21%)
  between operations  0.65 us (2%)
    pallas_call x1, Pallas kernels, per_device(): pl.pallas_call(functools.partial(kernel, blocks), out_shape=(jax.ShapeDty...  23.7 us
    unnamed x12, local copies, waits for them, and re-layouts  5.79 us
    reshape x1, local copies, waits for them, and re-layouts, per_device(): initial.reshape(1, half)  0.69 us

profile of v1, /device:TPU:0, one launch (start us, length us, event | category | flops | bytes accessed | tf_op | source)
XLA Modules:
  0.0 30.8 jit_solution(8729100096570501788)
XLA Ops:
  0.6 0.0 copy-start.4
  0.6 0.7 %reshape.7.init = bf16[1,512]{1,0:T(2,128)(2,1)S(1)} reshape(bf16[512]{0:T(512)(128)(2,1)} %param.10) | data formatting | bytes 2048 | tf_op jit(solution)/shard_map/reshape | solution.py:274
  1.3 0.0 copy-done.4
  1.3 0.0 copy-start
  1.3 1.2 %copy-done = f32[512,512]{1,0:T(8,128)S(1)} copy-done((f32[512,512]{1,0:T(8,128)S(1)}, f32[512,512]{1,0:T(8,128)}, u32[]{:S(2)}) %copy-start) | copy-done | bytes 1048600
  2.6 0.0 copy-start.1
  2.6 1.2 %copy-done.1 = f32[512,512]{1,0:T(8,128)S(1)} copy-done((f32[512,512]{1,0:T(8,128)S(1)}, f32[512,512]{1,0:T(8,128)}, u32[]{:S(2)}) %copy-start.1) | copy-done | bytes 1048600
  3.8 0.0 copy-start.2
  3.8 1.2 %copy-done.2 = bf16[512,1024]{1,0:T(8,128)(2,1)S(1)} copy-done((bf16[512,1024]{1,0:T(8,128)(2,1)S(1)}, bf16[512,1024]{1,0:T(8,128)(2,1)}, u32[]{:S(2)}) %copy-start.2) | copy-done | bytes 1048600
  5.0 0.0 copy-start.3
  5.0 0.9 %copy-done.3 = f32[4,16,512]{2,1,0:T(8,128)S(1)} copy-done((f32[4,16,512]{2,1,0:T(8,128)S(1)}, f32[4,16,512]{2,1,0:T(8,128)}, u32[]{:S(2)}) %copy-start.3) | copy-done | bytes 131096
  5.9 23.7 %shard_map.77 = (bf16[4,16,512]{2,1,0:T(8,128)(2,1)S(1)}, f32[4,8]{1,0:T(4,128)S(1)}) custom-call(f32[4,16,512]{2,1,0:T(8,128)S(1)} %copy-done.3, f32[512,512]{1,0:T(8,128)S(1)} %copy-done, f32[512,512]{1,0:T(8,128)S(1)} %copy-done.1, bf16[512,1024]{1,0:T(8,128)(2,1)S(1)} %copy-done.2, bf16[1,512]{1,0:T(2,128)(2,1)S(1)} %reshape.7.init, s32[4,16]{1,0:T(4,128)S(1)} %copy-done.4), custom_call_target="tpu_custom_call" | custom-call | tf_op jit(solution)/shard_map/pallas_call | solution.py:243
  29.6 0.6 %copy.10 = bf16[4,16,512]{2,1,0:T(8,128)(2,1)} copy(bf16[4,16,512]{2,1,0:T(8,128)(2,1)S(1)} %get-tuple-element.4) | data formatting | bytes 131072
  30.2 0.6 %copy.11 = f32[4,8]{1,0:T(4,128)} copy(f32[4,8]{1,0:T(4,128)S(1)} %get-tuple-element.5) | data formatting | bytes 256
Async XLA Ops:
  0.6 0.7 %copy-start.4 = (s32[4,16]{1,0:T(4,128)S(1)}, s32[4,16]{1,0:T(4,128)}, u32[]{:S(2)}) copy-start(s32[4,16]{1,0:T(4,128)} %flags.1) | copy-start | bytes 772
  1.3 1.2 %copy-start = (f32[512,512]{1,0:T(8,128)S(1)}, f32[512,512]{1,0:T(8,128)}, u32[]{:S(2)}) copy-start(f32[512,512]{1,0:T(8,128)} %means.1) | copy-start | bytes 3145732
  2.6 1.2 %copy-start.1 = (f32[512,512]{1,0:T(8,128)S(1)}, f32[512,512]{1,0:T(8,128)}, u32[]{:S(2)}) copy-start(f32[512,512]{1,0:T(8,128)} %prec.1) | copy-start | bytes 3145732
  3.8 1.2 %copy-start.2 = (bf16[512,1024]{1,0:T(8,128)(2,1)S(1)}, bf16[512,1024]{1,0:T(8,128)(2,1)}, u32[]{:S(2)}) copy-start(bf16[512,1024]{1,0:T(8,128)(2,1)} %trans.1) | copy-start | bytes 3145732
  5.0 0.9 %copy-start.3 = (f32[4,16,512]{2,1,0:T(8,128)S(1)}, f32[4,16,512]{2,1,0:T(8,128)}, u32[]{:S(2)}) copy-start(f32[4,16,512]{2,1,0:T(8,128)} %feat.1) | copy-start | bytes 393220

commit v2 on v1

--- a/solution.py
+++ b/solution.py
@@ -26,15 +26,20 @@
 
 
 def kernel(
-    blocks, feat, means, prec, trans, init, flags, post, evid,
-    xin, raw, wt, prior_in, w_hi, w_lo, sc, sc_in, em, xb, y, inv, flag_pad, mask, fin, fin_in,
-    send, recv,
+    blocks, feat, means_hbm, prec_hbm, trans, init_hbm, flags_hbm, post, evid,
+    means, prec, init, flags, xin, flag_in, raw, wt, lines, w_hi, w_lo, sc, halo, em, xb, y, inv, flag_pad, mask, fin, fin_in,
+    send, recv, load,
 ):
     c = lax.axis_index("tm")
     s = lax.axis_index("state")
     o = 1 - s
-    nxt = lax.rem(c + 1, blocks)
-    prv = lax.rem(c + blocks - 1, blocks)
+    target = c + 1 - 2 * s
+    source = c - 1 + 2 * s
+    has_target = jnp.logical_and(target >= 0, target < blocks)
+    has_source = jnp.logical_and(source >= 0, source < blocks)
+    has_next = c + 1 < blocks
+    has_prev = c > 0
+
     streams, frames, width = feat.shape
     half = trans.shape[0]
     states = trans.shape[1]
@@ -42,22 +47,42 @@
     chunk = min(256, states)
 
     barrier = pltpu.get_barrier_semaphore()
-    for who in ((nxt, s), (prv, s), (c, o)):
-        pl.semaphore_signal(barrier, inc=1, device_id=who, device_id_type=MESH)
+
+    @pl.when(has_source)
+    def _():
+        for core in range(2):
+            pl.semaphore_signal(barrier, inc=1, device_id=(source, core), device_id_type=MESH)
+
+    pl.semaphore_signal(barrier, inc=1, device_id=(c, o), device_id_type=MESH)
+
+    mine = pl.ds(pl.multiple_of(s * half, half), half)
+    theirs = pl.ds(pl.multiple_of(o * half, half), half)
+
+    loads = [
+        pltpu.make_async_copy(src, dst, load.at[k])
+        for k, (src, dst) in enumerate(
+            (
+                (flags_hbm, flags),
+                (init_hbm, init),
+                (prec_hbm, prec),
+                (means_hbm, means),
+                (trans, raw.at[mine]),
+                (feat, xin),
+            )
+        )
+    ]
+    for copy in loads:
+        copy.start()
 
     row_t = lax.broadcasted_iota(jnp.int32, (frames, frames), 0)
     col_t = lax.broadcasted_iota(jnp.int32, (frames, frames), 1)
+    loads[0].wait()
     for b in range(streams):
-        at = rows + b * frames
-        xin[at : at + frames, :width] = feat[b]
         line = jnp.broadcast_to(flags[b : b + 1, :].astype(F32), (frames, frames))
         column = jnp.sum(jnp.where(row_t == col_t, line, 0.0), axis=1, keepdims=True)
-        xin[at : at + frames, width:] = jnp.broadcast_to(column, (frames, LANES))
-    mine = pl.ds(pl.multiple_of(s * half, half), half)
-    theirs = pl.ds(pl.multiple_of(o * half, half), half)
-    prior_in[:, mine] = jnp.broadcast_to(init[...].astype(F32), (8, half))
-
-    pl.semaphore_wait(barrier, 3)
+        flag_in[o, b] = jnp.broadcast_to(column, (frames, LANES))
+    loads[1].wait()
+    lines[:, mine] = jnp.broadcast_to(init[...].astype(F32).reshape(1, half), (8, half))
 
     def remote(src, dst, k, who):
         return pltpu.make_async_remote_copy(
@@ -65,16 +90,18 @@
             device_id=who, device_id_type=MESH,
         )
 
-    own = xin.at[pl.ds(rows, rows)]
-    to_next = remote(own, xin.at[pl.ds(0, rows)], 0, (nxt, s))
-    to_prev = remote(own, xin.at[pl.ds(2 * rows, rows)], 1, (prv, s))
+    flag_copy = remote(flag_in.at[o], flag_in.at[s], 1, (target, s))
     trans_copy = remote(trans, raw.at[mine], 2, (c, o))
-    prior_copy = remote(prior_in.at[:, mine], prior_in.at[:, mine], 3, (c, o))
-    to_next.start()
-    to_prev.start()
-    trans_copy.start()
-    prior_copy.start()
-
+    line_copy = remote(lines.at[:, mine], lines.at[:, mine], 3, (c, o))
+    score_copy = remote(sc.at[s], sc.at[s], 4, (c, o))
+    next_copy = remote(sc.at[s], halo.at[s], 6 + s, (c + 1, 0))
+    prev_copy = pltpu.make_async_remote_copy(
+        src_ref=sc.at[s], dst_ref=halo.at[s], send_sem=send.at[0], recv_sem=recv.at[6 + s],
+        device_id=(c - 1, 1), device_id_type=MESH,
+    )
+
+    loads[2].wait()
+    loads[3].wait()
     p = prec[...]
     m = means[...]
     pm = p * m
@@ -86,29 +113,49 @@
     w_lo[:, width:] = lo
     offset = 0.5 * jnp.sum(jnp.log(p) - pm * m, axis=1, keepdims=True)
     offset = jnp.broadcast_to(offset, (half, LANES)).T[0:1]
-    raw[mine, :] = trans[...]
-
-    @pl.when(s == 1)
-    def _():
-        wt[:, half:] = trans[...].T
-
-    to_next.wait_recv()
-    to_prev.wait_recv()
-    x = xin[:, :width]
+    loads[5].wait()
+    x = xin[...].reshape(rows, width)
     sq_hi, sq_lo = split(x * x)
     x_hi, x_lo = split(x)
     left_hi = jnp.concatenate([sq_hi, x_hi], axis=1)
     left_lo = jnp.concatenate([sq_lo, x_lo], axis=1)
-    total = dot_t(left_hi, w_hi[...]) + (dot_t(left_lo, w_hi[...]) + dot_t(left_hi, w_lo[...]))
-    sc[...] = ACOUSTIC * (total + offset)
-
-    window = pl.ds(pl.multiple_of(s * rows, rows), 2 * rows)
-    other_window = pl.ds(pl.multiple_of(o * rows, rows), 2 * rows)
-    score_copy = remote(sc.at[other_window], sc_in, 4, (c, o))
+    both = dot_t(jnp.concatenate([left_hi, left_lo], axis=0), w_hi[...])
+    total = both[:rows] + (both[rows:] + dot_t(left_hi, w_lo[...]))
+    sc[s] = ACOUSTIC * (total + offset)
+
+    pl.semaphore_wait(barrier, 1 + has_next.astype(jnp.int32) + has_prev.astype(jnp.int32))
+
+    @pl.when(has_next)
+    def _():
+        next_copy.start()
+
+    @pl.when(has_prev)
+    def _():
+        prev_copy.start()
+
+    @pl.when(has_target)
+    def _():
+        flag_copy.start()
+
     score_copy.start()
-
+    line_copy.start()
+    trans_copy.start()
+    loads[4].wait()
+
+    @pl.when(s == 1)
+    def _():
+        wt[:, half:] = raw[half:, :].T
+
+    def emission(scores, at):
+        top = jnp.max(jnp.maximum(scores[0], scores[1]), axis=1, keepdims=True)
+        here = pl.ds(pl.multiple_of(at, rows), rows)
+        em[here, :half] = jnp.exp(scores[0] - top)
+        em[here, half:] = jnp.exp(scores[1] - top)
+
+    score_copy.wait_recv()
+    line_copy.wait_recv()
+    emission(sc, o * rows)
     trans_copy.wait_recv()
-    prior_copy.wait_recv()
 
     @pl.when(s == 1)
     def _():
@@ -117,19 +164,22 @@
     flag_pad[...] = jnp.ones_like(flag_pad)
     y[:, :PAD] = jnp.ones((streams, PAD, states), F32)
     y[:, PAD + 2 * frames :] = jnp.ones((streams, PAD, states), F32)
+
+    @pl.when(has_source)
+    def _():
+        flag_copy.wait_recv()
+        for core in range(2):
+            pltpu.make_async_copy(sc.at[core], halo.at[core], recv.at[6 + core]).wait()
+
+    @pl.when(jnp.logical_not(has_source))
+    def _():
+        flag_in[s] = jnp.ones((streams, frames, LANES), F32)
+        halo[...] = jnp.zeros_like(halo)
+
     for h in range(2):
         for b in range(streams):
-            at = pl.multiple_of((s + h) * rows + b * frames, frames)
-            flag_pad[b, PAD + h * frames : PAD + (h + 1) * frames] = xin[pl.ds(at, frames), width:]
-
-    score_copy.wait_recv()
-    for i in range(0, 2 * rows, 32):
-        at = pl.multiple_of(s * rows + i, 32)
-        a = sc[pl.ds(at, 32)]
-        z = sc_in[i : i + 32]
-        top = jnp.maximum(jnp.max(a, axis=1, keepdims=True), jnp.max(z, axis=1, keepdims=True))
-        em[i : i + 32, mine] = jnp.exp(a - top)
-        em[i : i + 32, theirs] = jnp.exp(z - top)
+            flag_pad[b, PAD + h * frames : PAD + (h + 1) * frames] = flag_in[h, b]
+    emission(halo, s * rows)
 
     pieces = [(h, b, (h * streams + b) * frames) for h in range(2) for b in range(streams)]
 
@@ -140,7 +190,7 @@
         d = -1 if forward else 1
         held = 1 if forward else 0
         if forward:
-            prior = prior_in[...]
+            prior = lines[...]
             prior = prior / jnp.sum(prior, axis=1, keepdims=True)
         else:
             prior = jnp.full((8, states), 1.0 / states, F32)
@@ -230,8 +280,20 @@
         line = jnp.sum(jnp.where(row_e == col_e, logs, 0.0), axis=0, keepdims=True)
         evid[b : b + 1, :] = line[:, :part]
 
-    for copy in (to_next, to_prev, trans_copy, prior_copy, score_copy, fin_copy):
+    for copy in (trans_copy, line_copy, score_copy, fin_copy):
         copy.wait_send()
+
+    @pl.when(has_target)
+    def _():
+        flag_copy.wait_send()
+
+    @pl.when(has_next)
+    def _():
+        next_copy.wait_send()
+
+    @pl.when(has_prev)
+    def _():
+        prev_copy.wait_send()
 
 
 def per_device(features, gauss_means, precisions, transitions, initial, reset_flags):
@@ -246,17 +308,22 @@
             jax.ShapeDtypeStruct((streams, frames, half), BF16),
             jax.ShapeDtypeStruct((streams, frames // 2), F32),
         ),
-        in_specs=[vmem] * 6,
+        in_specs=[pl.BlockSpec(memory_space=pltpu.HBM)] * 6,
         out_specs=(vmem, vmem),
         scratch_shapes=[
-            pltpu.VMEM((3 * rows, width + LANES), F32),
+            pltpu.VMEM((half, width), F32),
+            pltpu.VMEM((half, width), F32),
+            pltpu.VMEM((half,), BF16),
+            pltpu.VMEM((streams, frames), jnp.int32),
+            pltpu.VMEM((streams, frames, width), F32),
+            pltpu.VMEM((2, streams, frames, LANES), F32),
             pltpu.VMEM((states, states), BF16),
             pltpu.VMEM((states, states), BF16),
             pltpu.VMEM((8, states), F32),
             pltpu.VMEM((half, 2 * width), BF16),
             pltpu.VMEM((half, 2 * width), BF16),
-            pltpu.VMEM((3 * rows, half), F32),
-            pltpu.VMEM((2 * rows, half), F32),
+            pltpu.VMEM((2, rows, half), F32),
+            pltpu.VMEM((2, rows, half), F32),
             pltpu.VMEM((2 * rows, states), F32),
             pltpu.VMEM((2, 2 * rows, states), BF16),
             pltpu.VMEM((streams, 2 * frames + 2 * PAD, states), F32),
@@ -265,13 +332,14 @@
             pltpu.VMEM((2 * rows, LANES), F32),
             pltpu.VMEM((rows, states + LANES), F32),
             pltpu.VMEM((rows, states + LANES), F32),
-            pltpu.SemaphoreType.DMA((6,)),
+            pltpu.SemaphoreType.DMA((8,)),
+            pltpu.SemaphoreType.DMA((8,)),
             pltpu.SemaphoreType.DMA((6,)),
         ],
         compiler_params=pltpu.CompilerParams(
-            collective_id=0, has_side_effects=True, vmem_limit_bytes=40 * 1024 * 1024
+            collective_id=0, has_side_effects=True, vmem_limit_bytes=63 * 1024 * 1024
         ),
-    )(features, gauss_means, precisions, transitions, initial.reshape(1, half), reset_flags)
+    )(features, gauss_means, precisions, transitions, initial, reset_flags)
 
 
 def solution(mesh):

time: 31.1 us -> 24.9 us (0.80)
  local copies, waits for them, and re-layouts: 6.48 us -> 2.06 us
  Pallas kernels: 23.7 us -> 22.1 us
    unnamed x12 -> x4, local copies, waits for them, and re-layouts: 5.79 us -> 2.06 us
    pallas_call x1, Pallas kernels: 23.7 us -> 22.1 us  [per_device(): pl.pallas_call(functools.partial(kernel, blocks), out_shape=(jax.ShapeDty...]
    reshape x1 -> x0, local copies, waits for them, and re-layouts: 0.69 us -> none  [per_device(): initial.reshape(1, half)]
where the time goes in v2:
time: 24.9 us; the launch traced here: 24.8 us
  Pallas kernels  22.1 us (89%)
  local copies, waits for them, and re-layouts  2.06 us (8%)
  between operations  0.65 us (3%)
    pallas_call x1, Pallas kernels, per_device(): pl.pallas_call(functools.partial(kernel, blocks), out_shape=(jax.ShapeDty...  22.1 us
    unnamed x4, local copies, waits for them, and re-layouts  2.06 us

profile of v2, /device:TPU:0, one launch (start us, length us, event | category | flops | bytes accessed | tf_op | source)
XLA Modules:
  0.0 24.8 jit_solution(1056811249614553537)
XLA Ops:
  0.6 22.1 %shard_map.77 = (bf16[4,16,512]{2,1,0:T(8,128)(2,1)}, f32[4,8]{1,0:T(4,128)}) custom-call(f32[4,16,512]{2,1,0:T(8,128)} %feat.1, f32[512,512]{1,0:T(8,128)} %means_hbm.1, f32[512,512]{1,0:T(8,128)} %prec_hbm.1, bf16[512,1024]{1,0:T(8,128)(2,1)} %trans.1, bf16[512]{0:T(512)(128)(2,1)} %init_hbm.1, s32[4,16]{1,0:T(4,128)} %flags_hbm.1), custom_call_target="tpu_custom_call" | custom-call | tf_op jit(solution)/shard_map/pallas_call | solution.py:305
  22.7 0.0 copy-start
  22.7 1.5 %copy.10 = bf16[4,16,512]{2,1,0:T(8,128)(2,1)} copy(bf16[4,16,512]{2,1,0:T(8,128)(2,1)} %get-tuple-element.4) | data formatting | bytes 131072
  24.2 0.0 copy-done
  24.2 0.6 %copy.11 = f32[4,8]{1,0:T(4,128)} copy(f32[4,8]{1,0:T(4,128)S(1)} %copy-done) | data formatting | bytes 256
Async XLA Ops:
  22.7 1.5 %copy-start = (f32[4,8]{1,0:T(4,128)S(1)}, f32[4,8]{1,0:T(4,128)}, u32[]{:S(2)}) copy-start(f32[4,8]{1,0:T(4,128)} %get-tuple-element.5) | copy-start | bytes 388

commit v3 on v2

--- a/solution.py
+++ b/solution.py
@@ -27,7 +27,7 @@
 
 def kernel(
     blocks, feat, means_hbm, prec_hbm, trans, init_hbm, flags_hbm, post, evid,
-    means, prec, init, flags, xin, flag_in, raw, wt, lines, w_hi, w_lo, sc, halo, em, xb, y, inv, flag_pad, mask, fin, fin_in,
+    means, prec, init, flags, xin, flag_in, raw, wt, lines, w_hi, w_lo, sc, sent, halo, em, xb, y, inv, flag_pad, mask, fin, fin_in,
     send, recv, load,
 ):
     c = lax.axis_index("tm")
@@ -37,8 +37,6 @@
     source = c - 1 + 2 * s
     has_target = jnp.logical_and(target >= 0, target < blocks)
     has_source = jnp.logical_and(source >= 0, source < blocks)
-    has_next = c + 1 < blocks
-    has_prev = c > 0
 
     streams, frames, width = feat.shape
     half = trans.shape[0]
@@ -50,8 +48,7 @@
 
     @pl.when(has_source)
     def _():
-        for core in range(2):
-            pl.semaphore_signal(barrier, inc=1, device_id=(source, core), device_id_type=MESH)
+        pl.semaphore_signal(barrier, inc=1, device_id=(source, s), device_id_type=MESH)
 
     pl.semaphore_signal(barrier, inc=1, device_id=(c, o), device_id_type=MESH)
 
@@ -90,16 +87,10 @@
             device_id=who, device_id_type=MESH,
         )
 
-    flag_copy = remote(flag_in.at[o], flag_in.at[s], 1, (target, s))
+    halo_copy = remote(sent, halo, 0, (target, s))
     trans_copy = remote(trans, raw.at[mine], 2, (c, o))
     line_copy = remote(lines.at[:, mine], lines.at[:, mine], 3, (c, o))
     score_copy = remote(sc.at[s], sc.at[s], 4, (c, o))
-    next_copy = remote(sc.at[s], halo.at[s], 6 + s, (c + 1, 0))
-    prev_copy = pltpu.make_async_remote_copy(
-        src_ref=sc.at[s], dst_ref=halo.at[s], send_sem=send.at[0], recv_sem=recv.at[6 + s],
-        device_id=(c - 1, 1), device_id_type=MESH,
-    )
-
     loads[2].wait()
     loads[3].wait()
     p = prec[...]
@@ -123,22 +114,24 @@
     total = both[:rows] + (both[rows:] + dot_t(left_hi, w_lo[...]))
     sc[s] = ACOUSTIC * (total + offset)
 
-    pl.semaphore_wait(barrier, 1 + has_next.astype(jnp.int32) + has_prev.astype(jnp.int32))
-
-    @pl.when(has_next)
-    def _():
-        next_copy.start()
-
-    @pl.when(has_prev)
-    def _():
-        prev_copy.start()
-
-    @pl.when(has_target)
-    def _():
-        flag_copy.start()
-
+    pl.semaphore_wait(barrier, 1 + has_target.astype(jnp.int32))
     score_copy.start()
     line_copy.start()
+    for b in range(streams):
+        sent[b * frames : (b + 1) * frames, states:] = flag_in[o, b].astype(BF16)
+    score_copy.wait_recv()
+    top = jnp.max(jnp.maximum(sc[0], sc[1]), axis=1, keepdims=True)
+    here = pl.ds(pl.multiple_of(o * rows, rows), rows)
+    for core in range(2):
+        cols = slice(core * half, (core + 1) * half)
+        value = jnp.exp(sc[core] - top)
+        em[here, cols] = value
+        sent[:, cols] = value.astype(BF16)
+
+    @pl.when(has_target)
+    def _():
+        halo_copy.start()
+
     trans_copy.start()
     loads[4].wait()
 
@@ -146,15 +139,7 @@
     def _():
         wt[:, half:] = raw[half:, :].T
 
-    def emission(scores, at):
-        top = jnp.max(jnp.maximum(scores[0], scores[1]), axis=1, keepdims=True)
-        here = pl.ds(pl.multiple_of(at, rows), rows)
-        em[here, :half] = jnp.exp(scores[0] - top)
-        em[here, half:] = jnp.exp(scores[1] - top)
-
-    score_copy.wait_recv()
     line_copy.wait_recv()
-    emission(sc, o * rows)
     trans_copy.wait_recv()
 
     @pl.when(s == 1)
@@ -167,19 +152,18 @@
 
     @pl.when(has_source)
     def _():
-        flag_copy.wait_recv()
-        for core in range(2):
-            pltpu.make_async_copy(sc.at[core], halo.at[core], recv.at[6 + core]).wait()
+        halo_copy.wait_recv()
 
     @pl.when(jnp.logical_not(has_source))
     def _():
-        flag_in[s] = jnp.ones((streams, frames, LANES), F32)
-        halo[...] = jnp.zeros_like(halo)
-
+        halo[...] = jnp.ones_like(halo)
+
+    for b in range(streams):
+        flag_in[s, b] = halo[b * frames : (b + 1) * frames, states:].astype(F32)
     for h in range(2):
         for b in range(streams):
             flag_pad[b, PAD + h * frames : PAD + (h + 1) * frames] = flag_in[h, b]
-    emission(halo, s * rows)
+    em[pl.ds(pl.multiple_of(s * rows, rows), rows)] = halo[:, :states].astype(F32)
 
     pieces = [(h, b, (h * streams + b) * frames) for h in range(2) for b in range(streams)]
 
@@ -285,15 +269,7 @@
 
     @pl.when(has_target)
     def _():
-        flag_copy.wait_send()
-
-    @pl.when(has_next)
-    def _():
-        next_copy.wait_send()
-
-    @pl.when(has_prev)
-    def _():
-        prev_copy.wait_send()
+        halo_copy.wait_send()
 
 
 def per_device(features, gauss_means, precisions, transitions, initial, reset_flags):
@@ -323,7 +299,8 @@
             pltpu.VMEM((half, 2 * width), BF16),
             pltpu.VMEM((half, 2 * width), BF16),
             pltpu.VMEM((2, rows, half), F32),
-            pltpu.VMEM((2, rows, half), F32),
+            pltpu.VMEM((rows, states + LANES), BF16),
+            pltpu.VMEM((rows, states + LANES), BF16),
             pltpu.VMEM((2 * rows, states), F32),
             pltpu.VMEM((2, 2 * rows, states), BF16),
             pltpu.VMEM((streams, 2 * frames + 2 * PAD, states), F32),
@@ -332,8 +309,8 @@
             pltpu.VMEM((2 * rows, LANES), F32),
             pltpu.VMEM((rows, states + LANES), F32),
             pltpu.VMEM((rows, states + LANES), F32),
-            pltpu.SemaphoreType.DMA((8,)),
-            pltpu.SemaphoreType.DMA((8,)),
+            pltpu.SemaphoreType.DMA((6,)),
+            pltpu.SemaphoreType.DMA((6,)),
             pltpu.SemaphoreType.DMA((6,)),
         ],
         compiler_params=pltpu.CompilerParams(

time: 24.9 us -> 23.6 us (0.948)
  Pallas kernels: 22.1 us -> 20.7 us
    pallas_call x1, Pallas kernels: 22.1 us -> 20.7 us  [per_device(): pl.pallas_call(functools.partial(kernel, blocks), out_shape=(jax.ShapeDty...]
where the time goes in v3:
time: 23.6 us; the launch traced here: 23.4 us
  Pallas kernels  20.7 us (88%)
  local copies, waits for them, and re-layouts  2.06 us (9%)
  between operations  0.65 us (3%)
    pallas_call x1, Pallas kernels, per_device(): pl.pallas_call(functools.partial(kernel, blocks), out_shape=(jax.ShapeDty...  20.7 us
    unnamed x4, local copies, waits for them, and re-layouts  2.06 us

profile of v3, /device:TPU:0, one launch (start us, length us, event | category | flops | bytes accessed | tf_op | source)
XLA Modules:
  0.0 23.4 jit_solution(11452683159292563926)
XLA Ops:
  0.6 20.7 %shard_map.77 = (bf16[4,16,512]{2,1,0:T(8,128)(2,1)}, f32[4,8]{1,0:T(4,128)}) custom-call(f32[4,16,512]{2,1,0:T(8,128)} %feat.1, f32[512,512]{1,0:T(8,128)} %means_hbm.1, f32[512,512]{1,0:T(8,128)} %prec_hbm.1, bf16[512,1024]{1,0:T(8,128)(2,1)} %trans.1, bf16[512]{0:T(512)(128)(2,1)} %init_hbm.1, s32[4,16]{1,0:T(4,128)} %flags_hbm.1), custom_call_target="tpu_custom_call" | custom-call | tf_op jit(solution)/shard_map/pallas_call | solution.py:281
  21.3 0.0 copy-start
  21.4 1.5 %copy.10 = bf16[4,16,512]{2,1,0:T(8,128)(2,1)} copy(bf16[4,16,512]{2,1,0:T(8,128)(2,1)} %get-tuple-element.4) | data formatting | bytes 131072
  22.8 0.0 copy-done
  22.8 0.6 %copy.11 = f32[4,8]{1,0:T(4,128)} copy(f32[4,8]{1,0:T(4,128)S(1)} %copy-done) | data formatting | bytes 256
Async XLA Ops:
  21.3 1.5 %copy-start = (f32[4,8]{1,0:T(4,128)S(1)}, f32[4,8]{1,0:T(4,128)}, u32[]{:S(2)}) copy-start(f32[4,8]{1,0:T(4,128)} %get-tuple-element.5) | copy-start | bytes 388
